TPU v7x, 256 devices: a whole 4x4x8 slice. The times are simulated.
256 devices in a mesh: replica: 64 (over x, z_lo, y), fsdp: 4 (over z_hi, core).
Axes of the slice: x: 4, y: 4, z: 8 (z_hi: 2, z_lo: 4; z = z_hi * 4 + z_lo), core: 2. Of those that a mesh axis runs over, the one named last changes fastest.
Arguments:
- activations: bfloat16 [65536, 8192], P(('replica', 'fsdp')), may hold values from -6 to 6
- key_weight: bfloat16 [64, 8192, 512], P('replica', 'fsdp'), may hold values from -0.0625 to 0.0625
- key_cotangent: bfloat16 [65536, 512], P(('replica', 'fsdp')), may hold values from -0.5 to 0.5
- grad_codes: bfloat16 [64, 28672, 128], P('replica', 'fsdp'), may hold values from -1 to 1
- grad_scales: bfloat16 [64, 28672], P('replica', 'fsdp'), may hold values from 0.099609375 to 1
- master: float32 [28672, 128], P(('fsdp', 'replica')), may hold values from -5 to 5
- momentum: float32 [28672, 128], P(('fsdp', 'replica')), may hold values from -0.75 to 0.75
Outputs:
- key_rows: bfloat16 [65536, 512], P(('replica', 'fsdp'))
- weight_grad: bfloat16 [64, 8192, 512], P('replica', 'fsdp')
- new_master: float32 [28672, 128], P(('fsdp', 'replica'))
- new_momentum: float32 [28672, 128], P(('fsdp', 'replica'))
- new_codes: bfloat16 [28672, 128], P('fsdp')
- new_scales: bfloat16 [28672], P('fsdp')
All inputs are finite; a program needn't handle non-finite values. Where the computation divides by a largest or mean magnitude, that divisor is 1e-20 or more.
Results may differ from a plain program's by a relative error of at most 0.013.
Values may be sent and summed in bfloat16 or wider, within the bound.
A program may use at most 128 MiB of HBM per device.

v0:
```python
import jax
import jax.numpy as jnp
from jax import lax
from jax.sharding import PartitionSpec as P


def local(activations, key_weight, key_cotangent, grad_codes, grad_scales, master, momentum):
    local_rows = key_weight[0]
    columns = activations
    key_sums = jnp.dot(
        columns,
        lax.all_gather(local_rows, "fsdp", axis=0, tiled=True),
        preferred_element_type=jnp.float32,
    )
    columns = activations
    grad_sum = lax.psum_scatter(
        lax.dot_general(
            columns, key_cotangent, (((0,), (0,)), ((), ())), preferred_element_type=jnp.float32
        ).astype(jnp.bfloat16),
        "fsdp",
        scatter_dimension=0,
        tiled=True,
    )
    key_rows = key_sums.astype(jnp.bfloat16)
    weight_grad = grad_sum[None]
    replicas = lax.axis_size("replica")
    values = grad_codes[0].astype(jnp.float32) * grad_scales[0].astype(jnp.float32)[:, None]
    summed = lax.psum_scatter(values, "replica", scatter_dimension=0, tiled=True)
    outer_grad = summed / replicas
    new_momentum = 0.9 * momentum + outer_grad
    new_master = master - 0.7 * (outer_grad + 0.9 * new_momentum)
    group_scale = (jnp.max(jnp.abs(new_master), axis=1) + 1e-06).astype(jnp.bfloat16)
    own_codes = (new_master / group_scale.astype(jnp.float32)[:, None]).astype(jnp.bfloat16)
    new_codes, new_scales = (
        lax.all_gather(own_codes, "replica", axis=0, tiled=True),
        lax.all_gather(group_scale, "replica", axis=0, tiled=True),
    )
    return (key_rows, weight_grad, new_master, new_momentum, new_codes, new_scales)


def solution(mesh):
    return jax.shard_map(
        local,
        mesh=mesh,
        in_specs=(
            P(("replica", "fsdp"), None),
            P("replica", "fsdp", None),
            P(("replica", "fsdp"), None),
            P("replica", "fsdp", None),
            P("replica", "fsdp"),
            P(("fsdp", "replica"), None),
            P(("fsdp", "replica"), None),
        ),
        out_specs=(
            P(("replica", "fsdp"), None),
            P("replica", "fsdp", None),
            P(("fsdp", "replica"), None),
            P(("fsdp", "replica"), None),
            P("fsdp", None),
            P("fsdp"),
        ),
        check_vma=False,
    )
```

profile of v0, /device:TPU:1, one launch (start us, length us, event | category | flops | bytes accessed | tf_op | source)
XLA Modules:
  0.0 994.7 jit_solution(5105893493518903478)
XLA Ops:
  7.2 0.0 copy-start
  7.2 0.0 reduce-scatter.5.cloned.1.call-start
  7.2 0.8 convert_element_type.49
  8.0 0.0 copy-start.3
  8.1 0.0 copy-start.4
  8.1 5.4 convert_multiply_fusion
  13.5 0.0 reduce-scatter.5.cloned.1.call-update
  13.5 0.0 all-gather.4.cloned.1.call-start
  13.5 333.0 %reduce-scatter.5.cloned.1.call-done = f32[112,128]{1,0:T(8,128)} async-done(((f32[7168,128]{1,0:T(8,128)}), f32[112,128]{1,0:T(8,128)}) %reduce-scatter.5.cloned.1.call-update) | async-done | bytes 57360 | tf_op jit(solution)/shard_map/reduce_scatter | solution.py:28
  346.5 0.0 copy-done.3
  346.5 0.0 copy-done.4
  346.5 1.6 abs_reduce_fusion
  348.1 0.0 copy-start.2
  348.1 0.7 divide_convert_fusion
  348.8 0.0 all-gather.4.cloned.1.call-update
  348.8 0.0 all-gather.6.cloned.1.call-start
  348.9 0.7 all-gather.6.cloned.1.call-update
  349.6 0.0 reduce-scatter.3.cloned.1.call-start
  349.6 0.0 copy-done
  349.6 7.8 convolution_convert_fusion
  357.4 0.0 copy-done.2
  357.4 0.0 copy-start.5
  357.5 0.0 reduce-scatter.3.cloned.1.call-update
  357.5 0.6 copy-done.5
  358.1 0.6 dynamic-slice
  359.4 0.2 dynamic-update-slice
  359.6 310.3 %all-reduce = bf16[7168]{0:T(1024)(128)(2,1)} all-reduce(bf16[7168]{0:T(1024)(128)(2,1)S(1)} %dynamic-update-slice), channel_id=1, replica_groups=mesh['replica'=64,'fsdp'=4] {'replica'}, use_global_device_ids=true, to_apply=%add | all-reduce | flops 7168 | bytes 28672
  670.0 27.2 %all-gather.4.cloned.1.call-done = bf16[7168,128]{1,0:T(8,128)(2,1)} async-done(((bf16[112,128]{1,0:T(8,128)(2,1)}), bf16[7168,128]{1,0:T(8,128)(2,1)}) %all-gather.4.cloned.1.call-update) | async-done | bytes 1835024 | tf_op jit(solution)/shard_map/all_gather | solution.py:35
  697.1 0.0 copy-start.1
  697.1 158.2 %all-gather.6.cloned.1.call-done = bf16[1,8192,512]{2,1,0:T(8,128)(2,1)} async-done(((bf16[1,2048,512]{2,1,0:T(8,128)(2,1)}), bf16[1,8192,512]{2,1,0:T(8,128)(2,1)}) %all-gather.6.cloned.1.call-update) | async-done | bytes 8388624 | tf_op jit(solution)/shard_map/all_gather | solution.py:12
  855.3 7.7 fusion.2
  863.0 123.9 %reduce-scatter.3.cloned.1.call-done = bf16[2048,512]{1,0:T(8,128)(2,1)} async-done(((bf16[8192,512]{1,0:T(8,128)(2,1)}), bf16[2048,512]{1,0:T(8,128)(2,1)}) %reduce-scatter.3.cloned.1.call-update) | async-done | bytes 2097168 | tf_op jit(solution)/shard_map/reduce_scatter | solution.py:16
  986.9 0.0 copy-done.1
  986.9 1.2 copy.15
  (2 shorter events, 0.0 us)
Async XLA Ops:
  7.2 342.5 %copy-start = (bf16[256,512]{1,0:T(8,128)(2,1)S(1)}, bf16[256,512]{1,0:T(8,128)(2,1)}, u32[]{:S(2)}) copy-start(bf16[256,512]{1,0:T(8,128)(2,1)} %param.9) | copy-start | bytes 786436
  7.2 339.3 %reduce-scatter.5.cloned.1.call-start = ((), (), s32[]{:S(2)}) async-start(), calls=%async_computation.3 | async-start | bytes 3727360 | tf_op jit(solution)/shard_map/reduce_scatter | solution.py:28
  8.0 338.5 %copy-start.3 = (f32[112,128]{1,0:T(8,128)S(1)}, f32[112,128]{1,0:T(8,128)}, u32[]{:S(2)}) copy-start(f32[112,128]{1,0:T(8,128)} %param.12) | copy-start | bytes 172036
  8.1 338.5 %copy-start.4 = (f32[112,128]{1,0:T(8,128)S(1)}, f32[112,128]{1,0:T(8,128)}, u32[]{:S(2)}) copy-start(f32[112,128]{1,0:T(8,128)} %param.13) | copy-start | bytes 172036
  13.5 683.7 %all-gather.4.cloned.1.call-start = ((), (), s32[]{:S(2)}) async-start(), calls=%async_computation.4 | async-start | bytes 1863680 | tf_op jit(solution)/shard_map/all_gather | solution.py:35
  348.1 9.4 copy-start.2
  348.8 506.5 %all-gather.6.cloned.1.call-start = ((), (), s32[]{:S(2)}) async-start(), calls=%async_computation.5 | async-start | bytes 10485760 | tf_op jit(solution)/shard_map/all_gather | solution.py:12
  349.6 637.3 %reduce-scatter.3.cloned.1.call-start = ((), (), s32[]{:S(2)}) async-start(), calls=%async_computation.2 | async-start | bytes 10485760 | tf_op jit(solution)/shard_map/reduce_scatter | solution.py:16
  357.4 0.7 copy-start.5
  697.1 289.8 %copy-start.1 = (bf16[7168,128]{1,0:T(8,128)(2,1)S(1)}, bf16[7168,128]{1,0:T(8,128)(2,1)}, u32[]{:S(2)}) copy-start(bf16[7168,128]{1,0:T(8,128)(2,1)} %all-gather.4.cloned.1.call-done) | copy-start | bytes 5505028
Sparse Core Ops, SparseCore 0:
  13.6 332.8 reduce-scatter.4
  349.0 348.0 all-gather.3
  699.1 156.1 all-gather.5
  858.8 128.0 reduce-scatter.2
where the time goes:
time: 995 us
  waiting for transfers between devices  643 us (65%)
  blocking collectives  310 us (31%)
  matrix products  15.5 us (2%)
  between operations  14.5 us (1%)
    reduce_scatter x1, waiting for transfers between devices, local(): lax.psum_scatter(values, 'replica', scatter_dimension=0, tiled=True)  333 us
    unnamed x1, blocking collectives  310 us
    all_gather x1, waiting for transfers between devices, local(): lax.all_gather(local_rows, 'fsdp', axis=0, tiled=True)  158 us
    reduce_scatter x1, waiting for transfers between devices, local(): lax.psum_scatter(lax.dot_general(columns, key_cotangent, (((0,), (0,)), (...  124 us
    all_gather x1, waiting for transfers between devices, local(): lax.all_gather(own_codes, 'replica', axis=0, tiled=True)  27.2 us
  transfers between devices with their start and end apart: 4, of which 4 were waited for; matrix products, arithmetic and copies ran while one was open for 2% of the time, Pallas kernels for 0%

commit v1 on v0

v1 whole, which is shorter than its diff:
```python
import jax
import jax.numpy as jnp
from jax import lax
from jax.experimental import pallas as pl
from jax.experimental.pallas import tpu as pltpu
from jax.sharding import PartitionSpec as P

MESH = pl.DeviceIdType.MESH
F32, BF16 = jnp.float32, jnp.bfloat16

TOK, DEPTH, KW = 256, 2048, 512
CODE_ROWS, OWN = 7168, 112
QUARTER = CODE_ROWS // 4
CHUNKS = ((0, 64), (64, 64), (128, 64), (192, 64))
NQ = len(CHUNKS)


def kernel(
    act, weight, cot, codes, scales, master, momentum,
    key_out, grad_out, master_out, momentum_out, codes_out, scales_out,
    x_loc, x_rem, c_loc, c_rem, w_v, codes_v, scales_v, master_v, momentum_v,
    p_loc, p_sib, p_rem, p_ex, ret_s, ret_r, grad_f, grad_b, key_b,
    prod, recv_x, s_y, recv_y, s_z, recv_z, gath, nm_v, nmom_v,
    sem_in, sem_xs, sem_xr, sem_sib_s, sem_sib_r, sem_ex_s, sem_ex_r, sem_ret_s, sem_ret_r,
    sem_rs_s, sem_rs_r, sem_ag_s, sem_ag_r, sem_out,
):
    r = lax.axis_index("replica")
    f = lax.axis_index("fsdp")
    x, zl, y = r // 16, (r // 4) % 4, r % 4
    zh, c = f // 2, f % 2
    sib = (r, zh * 2 + (1 - c))
    far = [(r, (1 - zh) * 2 + k) for k in range(2)]
    far_same = (r, (1 - zh) * 2 + c)
    px = [(((x + k) % 4) * 16 + zl * 4 + y, f) for k in range(1, 4)]
    pz = [(x * 16 + ((zl + k) % 4) * 4 + y, f) for k in range(1, 4)]
    py = [(x * 16 + zl * 4 + (y + k) % 4, f) for k in range(1, 4)]

    def columns(owner):
        return pl.ds(pl.multiple_of(owner * DEPTH, DEPTH), DEPTH)

    def remote(src, dst, ssem, rsem, to):
        copy = pltpu.make_async_remote_copy(src, dst, ssem, rsem, device_id=to, device_id_type=MESH)
        copy.start()
        return copy

    def local_copy(src, dst, sem):
        copy = pltpu.make_async_copy(src, dst, sem)
        copy.start()
        return copy

    in_codes = local_copy(codes, codes_v, sem_in.at[0])
    in_scales = local_copy(scales, scales_v, sem_in.at[1])
    in_x = local_copy(act.at[:, columns(f)], x_loc.at[pl.ds(0, TOK)], sem_in.at[2])
    in_w = local_copy(weight, w_v, sem_in.at[3])
    in_c = local_copy(cot, c_loc.at[pl.ds(0, TOK)], sem_in.at[4])
    in_master = local_copy(master, master_v, sem_in.at[5])
    in_momentum = local_copy(momentum, momentum_v, sem_in.at[6])

    peers = [sib] + far + px + py + pz
    barrier = pltpu.get_barrier_semaphore()
    for peer in peers:
        pl.semaphore_signal(barrier, inc=1, device_id=peer, device_id_type=MESH)
    pl.semaphore_wait(barrier, len(peers))

    far_x = []
    for q, (start, rows) in enumerate(CHUNKS):
        for k in range(2):
            far_x.append(remote(
                act.at[pl.ds(start, rows), columns((1 - zh) * 2 + k)],
                x_rem.at[pl.ds(2 * start + c * rows, rows)],
                sem_xs.at[2 * q + k], sem_xr.at[2 * q + c], far[k],
            ))
    far_c = remote(cot, c_rem.at[pl.ds(c * TOK, TOK)], sem_sib_s.at[2], sem_sib_r.at[2], far_same)
    sib_x = remote(act.at[:, columns(zh * 2 + (1 - c))], x_loc.at[pl.ds(TOK, TOK)], sem_sib_s.at[0], sem_sib_r.at[0], sib)
    sib_c = remote(cot, c_loc.at[pl.ds(TOK, TOK)], sem_sib_s.at[1], sem_sib_r.at[1], sib)

    in_codes.wait()
    in_scales.wait()
    eye = lax.broadcasted_iota(jnp.int32, (128, 128), 0) == lax.broadcasted_iota(jnp.int32, (128, 128), 1)
    rs_x = []
    for k in (1, 3, 2, 0):
        base = ((x + k) % 4) * QUARTER

        def term(b, carry, k=k, base=base):
            at = pl.multiple_of(base + b * 128, 128)
            row = scales_v[:, pl.ds(at, 128)].astype(F32)
            diagonal = jnp.where(eye, jnp.broadcast_to(row, (128, 128)), 0.0).astype(BF16)
            block = jnp.dot(diagonal, codes_v[pl.ds(at, 128), :], preferred_element_type=F32)
            prod[k, pl.ds(pl.multiple_of(b * 128, 128), 128), :] = block.astype(BF16)
            return carry

        lax.fori_loop(0, QUARTER // 128, term, 0)
        if k:
            rs_x.append(remote(prod.at[k], recv_x.at[k - 1], sem_rs_s.at[k - 1], sem_rs_r.at[k - 1], px[k - 1]))

    in_x.wait()
    in_w.wait()
    in_c.wait()
    sib_x.wait()
    sib_c.wait()

    def keys_local(b, carry):
        at = pl.ds(pl.multiple_of(b * 128, 128), 128)
        p_loc[at, :] = jnp.dot(x_loc[at, :], w_v[...], preferred_element_type=F32)
        return carry

    lax.fori_loop(0, 2 * TOK // 128, keys_local, 0)
    sib_p = remote(p_loc.at[pl.ds(TOK, TOK)], p_sib, sem_sib_s.at[3], sem_sib_r.at[3], sib)

    def transposed_dot(lhs, rhs):
        return lax.dot_general(lhs, rhs, (((0,), (0,)), ((), ())), preferred_element_type=F32)

    def grad_local(b, carry):
        at = pl.ds(pl.multiple_of(b * 256, 256), 256)
        grad_f[at, :] = transposed_dot(x_loc[:, at], c_loc[...])
        return carry

    lax.fori_loop(0, DEPTH // 256, grad_local, 0)

    for copy in rs_x:
        copy.wait()

    def sum_x(b, carry):
        at = pl.ds(pl.multiple_of(b * OWN, 16), OWN)
        total = prod[0, at, :].astype(F32)
        for k in range(3):
            total += recv_x[k, at, :].astype(F32)
        s_y[b // 4, b % 4] = total.astype(BF16)
        return carry

    lax.fori_loop(0, 16, sum_x, 0)
    rs_y = [
        remote(s_y.at[:, (y + k) % 4], recv_y.at[k - 1], sem_rs_s.at[2 + k], sem_rs_r.at[2 + k], py[k - 1])
        for k in range(1, 4)
    ]
    for copy in rs_y:
        copy.wait()

    def sum_y(b, carry):
        total = s_y[b, y].astype(F32)
        for k in range(3):
            total += recv_y[k, b].astype(F32)
        s_z[b] = total.astype(BF16)
        return carry

    lax.fori_loop(0, 4, sum_y, 0)
    rs_z = [
        remote(s_z.at[(zl + k) % 4], recv_z.at[k - 1], sem_rs_s.at[5 + k], sem_rs_r.at[5 + k], pz[k - 1])
        for k in range(1, 4)
    ]
    in_master.wait()
    in_momentum.wait()
    for copy in rs_z:
        copy.wait()

    total = s_z[zl].astype(F32)
    for k in range(3):
        total += recv_z[k].astype(F32)
    outer = total / 64
    new_momentum = 0.9 * momentum_v[...] + outer
    new_master = master_v[...] - 0.7 * (outer + 0.9 * new_momentum)
    nmom_v[...] = new_momentum
    nm_v[...] = new_master
    largest = jnp.max(jnp.abs(new_master), axis=1, keepdims=True)
    scale = (largest + 1e-06).astype(BF16).astype(F32)
    gath[x, zl, y, 0:OWN, :] = (new_master / scale).astype(BF16)
    corner = lax.broadcasted_iota(jnp.int32, (OWN, 128), 0) == lax.broadcasted_iota(jnp.int32, (OWN, 128), 1)
    row = jnp.sum(jnp.where(corner, jnp.broadcast_to(scale, (OWN, 128)), 0.0), axis=0, keepdims=True)
    gath[x, zl, y, OWN:128, :] = jnp.broadcast_to(row, (128 - OWN, 128)).astype(BF16)
    out_master = local_copy(nm_v, master_out, sem_out.at[0])
    out_momentum = local_copy(nmom_v, momentum_out, sem_out.at[1])

    ag_z = [
        remote(gath.at[x, zl, y], gath.at[x, zl, y], sem_ag_s.at[k - 1], sem_ag_r.at[k - 1], pz[k - 1])
        for k in range(1, 4)
    ]
    for copy in ag_z:
        copy.wait()
    ag_y = [
        remote(gath.at[x, :, y], gath.at[x, :, y], sem_ag_s.at[2 + k], sem_ag_r.at[2 + k], py[k - 1])
        for k in range(1, 4)
    ]
    for copy in ag_y:
        copy.wait()
    ag_x = [
        remote(gath.at[x], gath.at[x], sem_ag_s.at[5 + k], sem_ag_r.at[5 + k], px[k - 1])
        for k in range(1, 4)
    ]

    def keys_far(q):
        start, rows = CHUNKS[q]
        for k in range(2):
            far_x[2 * q + k].wait_send()
        for k in range(2):
            pltpu.make_async_copy(
                x_rem.at[pl.ds(2 * start + k * rows, rows)], x_rem.at[pl.ds(2 * start + k * rows, rows)],
                sem_xr.at[2 * q + k],
            ).wait()
        both = pl.ds(2 * start, 2 * rows)
        p_rem[both, :] = jnp.dot(x_rem[both, :], w_v[...], preferred_element_type=F32)
        return remote(
            p_rem.at[pl.ds(2 * start + (1 - c) * rows, rows)], p_ex.at[pl.ds(start, rows)],
            sem_ex_s.at[q], sem_ex_r.at[q], sib,
        )

    def keys_back(q, exchange):
        start, rows = CHUNKS[q]
        exchange.wait()
        at = pl.ds(start, rows)
        mine = p_rem[pl.ds(pl.multiple_of(2 * start + c * rows, rows), rows), :]
        ret_s[at, :] = (mine + p_ex[at, :]).astype(BF16)
        return remote(ret_s.at[at], ret_r.at[at], sem_ret_s.at[q], sem_ret_r.at[q], far_same)

    returned = []
    for q in range(NQ - 1):
        exchange = keys_far(q)
        returned.append(keys_back(q, exchange))

    for copy in ag_x:
        copy.wait()
    out_codes = local_copy(gath.at[:, :, :, pl.ds(0, OWN)], codes_out, sem_out.at[2])
    out_scales = local_copy(gath.at[:, :, :, pl.ds(OWN, 16)], scales_out, sem_out.at[3])

    exchange = keys_far(NQ - 1)
    far_c.wait()
    share_c = remote(
        c_rem.at[pl.ds(c * TOK, TOK)], c_rem.at[pl.ds(c * TOK, TOK)], sem_sib_s.at[4], sem_sib_r.at[4], sib
    )
    returned.append(keys_back(NQ - 1, exchange))
    sib_p.wait()
    share_c.wait()

    def grad_far(b, carry):
        at = pl.ds(pl.multiple_of(b * 256, 256), 256)
        total = grad_f[at, :]
        for q, (start, rows) in enumerate(CHUNKS):
            for k in range(2):
                total += transposed_dot(x_rem[pl.ds(2 * start + k * rows, rows), at], c_rem[pl.ds(k * TOK + start, rows), :])
        grad_b[at, :] = total.astype(BF16)
        return carry

    lax.fori_loop(0, DEPTH // 256, grad_far, 0)
    out_grad = local_copy(grad_b, grad_out, sem_out.at[4])

    for q, (start, rows) in enumerate(CHUNKS):
        returned[q].wait()
        at = pl.ds(start, rows)
        key_b[at, :] = (p_loc[at, :] + p_sib[at, :] + ret_r[at, :].astype(F32)).astype(BF16)
    out_key = local_copy(key_b, key_out, sem_out.at[5])
    for copy in (out_master, out_momentum, out_codes, out_scales, out_grad, out_key):
        copy.wait()


def local(activations, key_weight, key_cotangent, grad_codes, grad_scales, master, momentum):
    anywhere = pl.BlockSpec(memory_space=pl.ANY)
    dma = pltpu.SemaphoreType.DMA
    key_rows, weight_grad, new_master, new_momentum, codes, scales = pl.pallas_call(
        kernel,
        out_shape=(
            jax.ShapeDtypeStruct((TOK, KW), BF16),
            jax.ShapeDtypeStruct((DEPTH, KW), BF16),
            jax.ShapeDtypeStruct((OWN, 128), F32),
            jax.ShapeDtypeStruct((OWN, 128), F32),
            jax.ShapeDtypeStruct((4, 4, 4, OWN, 128), BF16),
            jax.ShapeDtypeStruct((4, 4, 4, 16, 128), BF16),
        ),
        in_specs=[anywhere] * 7,
        out_specs=(anywhere,) * 6,
        scratch_shapes=[
            pltpu.VMEM((2 * TOK, DEPTH), BF16),
            pltpu.VMEM((2 * TOK, DEPTH), BF16),
            pltpu.VMEM((2 * TOK, KW), BF16),
            pltpu.VMEM((2 * TOK, KW), BF16),
            pltpu.VMEM((DEPTH, KW), BF16),
            pltpu.VMEM((CODE_ROWS, 128), BF16),
            pltpu.VMEM((1, CODE_ROWS), BF16),
            pltpu.VMEM((OWN, 128), F32),
            pltpu.VMEM((OWN, 128), F32),
            pltpu.VMEM((2 * TOK, KW), F32),
            pltpu.VMEM((TOK, KW), F32),
            pltpu.VMEM((2 * TOK, KW), F32),
            pltpu.VMEM((TOK, KW), F32),
            pltpu.VMEM((TOK, KW), BF16),
            pltpu.VMEM((TOK, KW), BF16),
            pltpu.VMEM((DEPTH, KW), F32),
            pltpu.VMEM((DEPTH, KW), BF16),
            pltpu.VMEM((TOK, KW), BF16),
            pltpu.VMEM((4, QUARTER, 128), BF16),
            pltpu.VMEM((3, QUARTER, 128), BF16),
            pltpu.VMEM((4, 4, OWN, 128), BF16),
            pltpu.VMEM((3, 4, OWN, 128), BF16),
            pltpu.VMEM((4, OWN, 128), BF16),
            pltpu.VMEM((3, OWN, 128), BF16),
            pltpu.VMEM((4, 4, 4, 128, 128), BF16),
            pltpu.VMEM((OWN, 128), F32),
            pltpu.VMEM((OWN, 128), F32),
            dma((7,)),
            dma((2 * NQ,)), dma((2 * NQ,)),
            dma((5,)), dma((5,)),
            dma((NQ,)), dma((NQ,)),
            dma((NQ,)), dma((NQ,)),
            dma((9,)), dma((9,)),
            dma((9,)), dma((9,)),
            dma((6,)),
        ],
        compiler_params=pltpu.CompilerParams(
            collective_id=0, has_side_effects=True, vmem_limit_bytes=48 * 2**20
        ),
    )(activations, key_weight[0], key_cotangent, grad_codes[0], grad_scales, master, momentum)
    new_codes = codes.reshape(CODE_ROWS, 128)
    new_scales = scales[:, :, :, 0, :OWN].reshape(CODE_ROWS)
    return (key_rows, weight_grad[None], new_master, new_momentum, new_codes, new_scales)


def solution(mesh):
    return jax.shard_map(
        local,
        mesh=mesh,
        in_specs=(
            P(("replica", "fsdp"), None),
            P("replica", "fsdp", None),
            P(("replica", "fsdp"), None),
            P("replica", "fsdp", None),
            P("replica", "fsdp"),
            P(("fsdp", "replica"), None),
            P(("fsdp", "replica"), None),
        ),
        out_specs=(
            P(("replica", "fsdp"), None),
            P("replica", "fsdp", None),
            P(("fsdp", "replica"), None),
            P(("fsdp", "replica"), None),
            P("fsdp", None),
            P("fsdp"),
        ),
        check_vma=False,
    )
```

time: 995 us -> 176 us (0.18)
  waiting for transfers between devices: 643 us -> 0 us
  blocking collectives: 310 us -> 0 us
  Pallas kernels: 0 us -> 163 us
  matrix products: 15.5 us -> 0 us
  between operations: 14.5 us -> 0.66 us
    reduce_scatter x2 -> x0, waiting for transfers between devices: 457 us -> none  [the longest x1 333 us: local(): lax.psum_scatter(values, 'replica', scatter_dimension=0, tiled=True)]
    unnamed x1 -> x0, blocking collectives: 310 us -> none
    all_gather x2 -> x0, waiting for transfers between devices: 185 us -> none  [the longest x1 158 us: local(): lax.all_gather(local_rows, 'fsdp', axis=0, tiled=True)]
    pallas_call x0 -> x1, Pallas kernels: none -> 163 us  [local(): pl.pallas_call(kernel, out_shape=(jax.ShapeDtypeStruct((TOK, KW), BF16),...]
    dot_general x2 -> x0, matrix products: 15.5 us -> none  [the longest x1 7.81 us: local(): lax.dot_general(columns, key_cotangent, (((0,), (0,)), ((), ())), preferr...]
  transfers between devices with their start and end apart: 4 -> 0, of which waited for: 4 -> 0; matrix products, arithmetic and copies ran while one was open for 2% -> 0% of each run, Pallas kernels for 0% -> 0%
where the time goes in v1:
time: 176 us; the launch traced here: 175 us
  Pallas kernels  163 us (93%)
  local copies, waits for them, and re-layouts  11.8 us (7%)
    pallas_call x1, Pallas kernels, local(): pl.pallas_call(kernel, out_shape=(jax.ShapeDtypeStruct((TOK, KW), BF16),...  163 us
    unnamed x15, local copies, waits for them, and re-layouts  11 us

profile of v1, /device:TPU:1, one launch (start us, length us, event | category | flops | bytes accessed | tf_op | source)
XLA Modules:
  0.0 175.2 jit_solution(10741404436058574553)
XLA Ops:
  0.6 0.0 copy-start
  0.6 1.5 copy-done
  2.1 0.0 copy-start.1
  2.1 0.9 copy-done.1
  3.1 0.0 copy-start.2
  3.1 0.8 copy-done.2
  3.9 0.0 copy-start.3
  3.9 0.8 copy-done.3
  4.7 0.0 copy-start.4
  4.7 0.7 copy-done.4
  5.5 162.7 %shard_map.118 = (bf16[256,512]{1,0:T(8,128)(2,1)S(1)}, bf16[2048,512]{1,0:T(8,128)(2,1)}, f32[112,128]{1,0:T(8,128)S(1)}, f32[112,128]{1,0:T(8,128)S(1)}, bf16[...) custom-call(bf16[256,8192]{1,0:T(8,128)(2,1)} %act.1, bf16[2048,512]{1,0:T(8,128)(2,1)} %bitcast.6, ...), custom_call_target="tpu_custom_call" | custom-call | tf_op jit(solution)/shard_map/pallas_call | solution.py:257
  168.1 0.1 slice_reduce_fusion
  168.3 0.7 reshape_squeeze.3
  169.0 0.7 copy.18
  169.7 3.0 %copy.19 = bf16[1,2048,512]{2,1,0:T(8,128)(2,1)} copy(bf16[1,2048,512]{2,1,0:T(8,128)(2,1)} %bitcast.7) | data formatting | bytes 4194304
  172.7 0.6 copy.20
  173.3 0.6 copy.21
  173.9 1.2 copy.22
Async XLA Ops:
  0.6 1.5 copy-start
  2.1 0.9 copy-start.1
  3.1 0.8 copy-start.2
  3.9 0.8 copy-start.3
  4.7 0.7 copy-start.4

commit v2 on v1

--- a/solution.py
+++ b/solution.py
@@ -11,18 +11,22 @@
 TOK, DEPTH, KW = 256, 2048, 512
 CODE_ROWS, OWN = 7168, 112
 QUARTER = CODE_ROWS // 4
-CHUNKS = ((0, 64), (64, 64), (128, 64), (192, 64))
+UNIT, WINDOW = 16, 2
+NU = TOK // UNIT
+CHUNKS = ((0, 64), (64, 64), (128, 64), (192, 32), (224, 32))
 NQ = len(CHUNKS)
+ORDER = [*range(0, 4), "c", *range(4, NU)]
+PUMPS = (1, 0, 1, 2, 1, 1, 1, 1, 3, 0)
 
 
 def kernel(
     act, weight, cot, codes, scales, master, momentum,
-    key_out, grad_out, master_out, momentum_out, codes_out, scales_out,
-    x_loc, x_rem, c_loc, c_rem, w_v, codes_v, scales_v, master_v, momentum_v,
-    p_loc, p_sib, p_rem, p_ex, ret_s, ret_r, grad_f, grad_b, key_b,
-    prod, recv_x, s_y, recv_y, s_z, recv_z, gath, nm_v, nmom_v,
+    key_b, grad_b, nm_v, nmom_v, gath, scales_b,
+    x_loc, x_rem, c_loc, c_rem, c_mix, w_v, codes_v, scales_v, master_v, momentum_v,
+    p_loc, p_sib, p_rem, p_ex, ret_s, ret_r, grad_f,
+    prod, recv_x, s_y, recv_y, s_z, recv_z,
     sem_in, sem_xs, sem_xr, sem_sib_s, sem_sib_r, sem_ex_s, sem_ex_r, sem_ret_s, sem_ret_r,
-    sem_rs_s, sem_rs_r, sem_ag_s, sem_ag_r, sem_out,
+    sem_rs_s, sem_rs_r, sem_ag_s, sem_ag_r,
 ):
     r = lax.axis_index("replica")
     f = lax.axis_index("fsdp")
@@ -62,15 +66,33 @@
         pl.semaphore_signal(barrier, inc=1, device_id=peer, device_id_type=MESH)
     pl.semaphore_wait(barrier, len(peers))
 
-    far_x = []
-    for q, (start, rows) in enumerate(CHUNKS):
+    far_x, far_c, issued = {}, [], []
+
+    def send_far(u):
+        if u == "c":
+            copy = remote(cot, c_rem.at[pl.ds(c * TOK, TOK)], sem_sib_s.at[2], sem_sib_r.at[2], far_same)
+            far_c.append(copy)
+            return [copy]
+        start, rows = next(chunk for chunk in CHUNKS if chunk[0] <= u * UNIT < sum(chunk))
+        copies = []
         for k in range(2):
-            far_x.append(remote(
-                act.at[pl.ds(start, rows), columns((1 - zh) * 2 + k)],
-                x_rem.at[pl.ds(2 * start + c * rows, rows)],
-                sem_xs.at[2 * q + k], sem_xr.at[2 * q + c], far[k],
+            copies.append(remote(
+                act.at[pl.ds(u * UNIT, UNIT), columns((1 - zh) * 2 + k)],
+                x_rem.at[pl.ds(start + u * UNIT + c * rows, UNIT)],
+                sem_xs.at[2 * u + k], sem_xr.at[2 * u + c], far[k],
             ))
-    far_c = remote(cot, c_rem.at[pl.ds(c * TOK, TOK)], sem_sib_s.at[2], sem_sib_r.at[2], far_same)
+        return copies
+
+    def pump(steps):
+        for _ in range(steps):
+            if len(issued) == len(ORDER):
+                return
+            if len(issued) >= WINDOW:
+                for copy in issued[len(issued) - WINDOW]:
+                    copy.wait_send()
+            issued.append(send_far(ORDER[len(issued)]))
+
+    pump(WINDOW)
     sib_x = remote(act.at[:, columns(zh * 2 + (1 - c))], x_loc.at[pl.ds(TOK, TOK)], sem_sib_s.at[0], sem_sib_r.at[0], sib)
     sib_c = remote(cot, c_loc.at[pl.ds(TOK, TOK)], sem_sib_s.at[1], sem_sib_r.at[1], sib)
 
@@ -92,7 +114,10 @@
         lax.fori_loop(0, QUARTER // 128, term, 0)
         if k:
             rs_x.append(remote(prod.at[k], recv_x.at[k - 1], sem_rs_s.at[k - 1], sem_rs_r.at[k - 1], px[k - 1]))
-
+        if k in (2, 3):
+            pump(PUMPS[0])
+
+    pump(PUMPS[1])
     in_x.wait()
     in_w.wait()
     in_c.wait()
@@ -107,6 +132,8 @@
     lax.fori_loop(0, 2 * TOK // 128, keys_local, 0)
     sib_p = remote(p_loc.at[pl.ds(TOK, TOK)], p_sib, sem_sib_s.at[3], sem_sib_r.at[3], sib)
 
+    pump(PUMPS[2])
+
     def transposed_dot(lhs, rhs):
         return lax.dot_general(lhs, rhs, (((0,), (0,)), ((), ())), preferred_element_type=F32)
 
@@ -117,6 +144,7 @@
 
     lax.fori_loop(0, DEPTH // 256, grad_local, 0)
 
+    pump(PUMPS[3])
     for copy in rs_x:
         copy.wait()
 
@@ -133,6 +161,7 @@
         remote(s_y.at[:, (y + k) % 4], recv_y.at[k - 1], sem_rs_s.at[2 + k], sem_rs_r.at[2 + k], py[k - 1])
         for k in range(1, 4)
     ]
+    pump(PUMPS[4])
     for copy in rs_y:
         copy.wait()
 
@@ -148,6 +177,7 @@
         remote(s_z.at[(zl + k) % 4], recv_z.at[k - 1], sem_rs_s.at[5 + k], sem_rs_r.at[5 + k], pz[k - 1])
         for k in range(1, 4)
     ]
+    pump(PUMPS[5])
     in_master.wait()
     in_momentum.wait()
     for copy in rs_z:
@@ -167,19 +197,19 @@
     corner = lax.broadcasted_iota(jnp.int32, (OWN, 128), 0) == lax.broadcasted_iota(jnp.int32, (OWN, 128), 1)
     row = jnp.sum(jnp.where(corner, jnp.broadcast_to(scale, (OWN, 128)), 0.0), axis=0, keepdims=True)
     gath[x, zl, y, OWN:128, :] = jnp.broadcast_to(row, (128 - OWN, 128)).astype(BF16)
-    out_master = local_copy(nm_v, master_out, sem_out.at[0])
-    out_momentum = local_copy(nmom_v, momentum_out, sem_out.at[1])
 
     ag_z = [
         remote(gath.at[x, zl, y], gath.at[x, zl, y], sem_ag_s.at[k - 1], sem_ag_r.at[k - 1], pz[k - 1])
         for k in range(1, 4)
     ]
+    pump(PUMPS[6])
     for copy in ag_z:
         copy.wait()
     ag_y = [
         remote(gath.at[x, :, y], gath.at[x, :, y], sem_ag_s.at[2 + k], sem_ag_r.at[2 + k], py[k - 1])
         for k in range(1, 4)
     ]
+    pump(PUMPS[7])
     for copy in ag_y:
         copy.wait()
     ag_x = [
@@ -187,15 +217,36 @@
         for k in range(1, 4)
     ]
 
+    pump(PUMPS[8])
+    far_c[0].wait_recv()
+    share_c = remote(
+        c_rem.at[pl.ds(c * TOK, TOK)], c_rem.at[pl.ds(c * TOK, TOK)], sem_sib_s.at[4], sem_sib_r.at[4], sib
+    )
+
+    def pack_scales():
+        lane = lax.broadcasted_iota(jnp.int32, (1, 128), 1)
+        for part in range(4):
+            rows = [jnp.zeros((1, 128), F32) for _ in range(QUARTER // 128)]
+            for owner in range(16):
+                at, shift = divmod(owner * OWN, 128)
+                row = gath[part, owner // 4, owner % 4, pl.ds(OWN, 16), :][0:1].astype(F32)
+                row = jnp.where(lane < OWN, row, 0.0)
+                if shift:
+                    row = pltpu.roll(row, shift, 1)
+                rows[at] += jnp.where(lane >= shift, row, 0.0)
+                if shift + OWN > 128:
+                    rows[at + 1] += jnp.where(lane < shift, row, 0.0)
+            for i, row in enumerate(rows):
+                scales_b[pl.ds(part * (QUARTER // 128) + i, 1), :] = row
+
     def keys_far(q):
         start, rows = CHUNKS[q]
-        for k in range(2):
-            far_x[2 * q + k].wait_send()
-        for k in range(2):
-            pltpu.make_async_copy(
-                x_rem.at[pl.ds(2 * start + k * rows, rows)], x_rem.at[pl.ds(2 * start + k * rows, rows)],
-                sem_xr.at[2 * q + k],
-            ).wait()
+        for u in range(start // UNIT, (start + rows) // UNIT):
+            while u not in [item for item in ORDER[:len(issued)]]:
+                pump(1)
+            for k in range(2):
+                part = x_rem.at[pl.ds(start + u * UNIT + k * rows, UNIT)]
+                pltpu.make_async_copy(part, part, sem_xr.at[2 * u + k]).wait()
         both = pl.ds(2 * start, 2 * rows)
         p_rem[both, :] = jnp.dot(x_rem[both, :], w_v[...], preferred_element_type=F32)
         return remote(
@@ -211,64 +262,93 @@
         ret_s[at, :] = (mine + p_ex[at, :]).astype(BF16)
         return remote(ret_s.at[at], ret_r.at[at], sem_ret_s.at[q], sem_ret_r.at[q], far_same)
 
+    def grad_far(q):
+        start, rows = CHUNKS[q]
+        both = pl.ds(2 * start, 2 * rows)
+
+        def tile(b, carry):
+            at = pl.ds(pl.multiple_of(b * 256, 256), 256)
+            total = grad_f[at, :] + transposed_dot(x_rem[both, at], c_mix[both, :])
+            if q < NQ - 1:
+                grad_f[at, :] = total
+            else:
+                grad_b[at, :] = total.astype(BF16)
+            return carry
+
+        lax.fori_loop(0, DEPTH // 256, tile, 0)
+
+    exchange = keys_far(0)
+    share_c.wait()
+    for q, (start, rows) in enumerate(CHUNKS):
+        for k in range(2):
+            c_mix[pl.ds(2 * start + k * rows, rows), :] = c_rem[pl.ds(k * TOK + start, rows), :]
     returned = []
-    for q in range(NQ - 1):
-        exchange = keys_far(q)
-        returned.append(keys_back(q, exchange))
-
-    for copy in ag_x:
-        copy.wait()
-    out_codes = local_copy(gath.at[:, :, :, pl.ds(0, OWN)], codes_out, sem_out.at[2])
-    out_scales = local_copy(gath.at[:, :, :, pl.ds(OWN, 16)], scales_out, sem_out.at[3])
-
-    exchange = keys_far(NQ - 1)
-    far_c.wait()
-    share_c = remote(
-        c_rem.at[pl.ds(c * TOK, TOK)], c_rem.at[pl.ds(c * TOK, TOK)], sem_sib_s.at[4], sem_sib_r.at[4], sib
-    )
+    pump(PUMPS[9])
+    for q in range(NQ):
+        if q == NQ - 2:
+            for copy in ag_x:
+                copy.wait()
+            pack_scales()
+        if q:
+            exchange = keys_far(q)
+        if q < NQ - 1:
+            grad_far(q)
+            pump(1)
+            returned.append(keys_back(q, exchange))
+            pump(1)
     returned.append(keys_back(NQ - 1, exchange))
+    grad_far(NQ - 1)
+    for copies in issued[-WINDOW:]:
+        for copy in copies:
+            copy.wait_send()
     sib_p.wait()
-    share_c.wait()
-
-    def grad_far(b, carry):
-        at = pl.ds(pl.multiple_of(b * 256, 256), 256)
-        total = grad_f[at, :]
-        for q, (start, rows) in enumerate(CHUNKS):
-            for k in range(2):
-                total += transposed_dot(x_rem[pl.ds(2 * start + k * rows, rows), at], c_rem[pl.ds(k * TOK + start, rows), :])
-        grad_b[at, :] = total.astype(BF16)
-        return carry
-
-    lax.fori_loop(0, DEPTH // 256, grad_far, 0)
-    out_grad = local_copy(grad_b, grad_out, sem_out.at[4])
 
     for q, (start, rows) in enumerate(CHUNKS):
         returned[q].wait()
         at = pl.ds(start, rows)
         key_b[at, :] = (p_loc[at, :] + p_sib[at, :] + ret_r[at, :].astype(F32)).astype(BF16)
-    out_key = local_copy(key_b, key_out, sem_out.at[5])
-    for copy in (out_master, out_momentum, out_codes, out_scales, out_grad, out_key):
+
+
+def write(key_v, grad_v, nm_v, nmom_v, gath, scales_v, key_out, grad_out, master_out, momentum_out, codes_out, scales_out, scales_b, sem):
+    copies = [
+        pltpu.make_async_copy(src, dst, sem.at[i])
+        for i, (src, dst) in enumerate((
+            (grad_v, grad_out),
+            (gath.at[:, :, :, pl.ds(0, OWN)], codes_out),
+            (key_v, key_out),
+            (nm_v, master_out),
+            (nmom_v, momentum_out),
+            (scales_b, scales_out),
+        ))
+    ]
+    for copy in copies[:-1]:
+        copy.start()
+    scales_b[...] = scales_v[...].astype(BF16)
+    copies[-1].start()
+    for copy in copies:
         copy.wait()
 
 
 def local(activations, key_weight, key_cotangent, grad_codes, grad_scales, master, momentum):
-    anywhere = pl.BlockSpec(memory_space=pl.ANY)
+    anywhere, in_hbm = pl.BlockSpec(memory_space=pl.ANY), pl.BlockSpec(memory_space=pltpu.HBM)
+    in_vmem = pl.BlockSpec(memory_space=pltpu.VMEM)
     dma = pltpu.SemaphoreType.DMA
-    key_rows, weight_grad, new_master, new_momentum, codes, scales = pl.pallas_call(
+    results = pl.pallas_call(
         kernel,
         out_shape=(
-            jax.ShapeDtypeStruct((TOK, KW), BF16),
-            jax.ShapeDtypeStruct((DEPTH, KW), BF16),
-            jax.ShapeDtypeStruct((OWN, 128), F32),
-            jax.ShapeDtypeStruct((OWN, 128), F32),
-            jax.ShapeDtypeStruct((4, 4, 4, OWN, 128), BF16),
-            jax.ShapeDtypeStruct((4, 4, 4, 16, 128), BF16),
+            pltpu.VMEM((TOK, KW), BF16),
+            pltpu.VMEM((DEPTH, KW), BF16),
+            pltpu.VMEM((OWN, 128), F32),
+            pltpu.VMEM((OWN, 128), F32),
+            pltpu.VMEM((4, 4, 4, 128, 128), BF16),
+            pltpu.VMEM((CODE_ROWS // 128, 128), F32),
         ),
-        in_specs=[anywhere] * 7,
-        out_specs=(anywhere,) * 6,
+        in_specs=[in_hbm] * 7,
+        out_specs=(in_vmem,) * 6,
         scratch_shapes=[
             pltpu.VMEM((2 * TOK, DEPTH), BF16),
             pltpu.VMEM((2 * TOK, DEPTH), BF16),
+            pltpu.VMEM((2 * TOK, KW), BF16),
             pltpu.VMEM((2 * TOK, KW), BF16),
             pltpu.VMEM((2 * TOK, KW), BF16),
             pltpu.VMEM((DEPTH, KW), BF16),
@@ -283,32 +363,40 @@
             pltpu.VMEM((TOK, KW), BF16),
             pltpu.VMEM((TOK, KW), BF16),
             pltpu.VMEM((DEPTH, KW), F32),
-            pltpu.VMEM((DEPTH, KW), BF16),
-            pltpu.VMEM((TOK, KW), BF16),
             pltpu.VMEM((4, QUARTER, 128), BF16),
             pltpu.VMEM((3, QUARTER, 128), BF16),
             pltpu.VMEM((4, 4, OWN, 128), BF16),
             pltpu.VMEM((3, 4, OWN, 128), BF16),
             pltpu.VMEM((4, OWN, 128), BF16),
             pltpu.VMEM((3, OWN, 128), BF16),
-            pltpu.VMEM((4, 4, 4, 128, 128), BF16),
-            pltpu.VMEM((OWN, 128), F32),
-            pltpu.VMEM((OWN, 128), F32),
             dma((7,)),
-            dma((2 * NQ,)), dma((2 * NQ,)),
+            dma((2 * NU,)), dma((2 * NU,)),
             dma((5,)), dma((5,)),
             dma((NQ,)), dma((NQ,)),
             dma((NQ,)), dma((NQ,)),
             dma((9,)), dma((9,)),
             dma((9,)), dma((9,)),
-            dma((6,)),
         ],
         compiler_params=pltpu.CompilerParams(
-            collective_id=0, has_side_effects=True, vmem_limit_bytes=48 * 2**20
+            collective_id=0, has_side_effects=True, vmem_limit_bytes=58 * 2**20
         ),
     )(activations, key_weight[0], key_cotangent, grad_codes[0], grad_scales, master, momentum)
-    new_codes = codes.reshape(CODE_ROWS, 128)
-    new_scales = scales[:, :, :, 0, :OWN].reshape(CODE_ROWS)
+    key_rows, weight_grad, new_master, new_momentum, codes, scales = pl.pallas_call(
+        write,
+        out_shape=(
+            jax.ShapeDtypeStruct((TOK, KW), BF16),
+            jax.ShapeDtypeStruct((DEPTH, KW), BF16),
+            jax.ShapeDtypeStruct((OWN, 128), F32),
+            jax.ShapeDtypeStruct((OWN, 128), F32),
+            jax.ShapeDtypeStruct((4, 4, 4, OWN, 128), BF16),
+            jax.ShapeDtypeStruct((CODE_ROWS // 128, 128), BF16),
+        ),
+        in_specs=[in_vmem] * 6,
+        out_specs=(anywhere,) * 6,
+        scratch_shapes=[pltpu.VMEM((CODE_ROWS // 128, 128), BF16), dma((6,))],
+        compiler_params=pltpu.CompilerParams(vmem_limit_bytes=2 * 2**20),
+    )(*[pltpu.with_memory_space_constraint(v, pltpu.VMEM) for v in results])
+    new_codes, new_scales = codes.reshape(CODE_ROWS, 128), scales.reshape(CODE_ROWS)
     return (key_rows, weight_grad[None], new_master, new_momentum, new_codes, new_scales)
 
 

time: 176 us -> 144 us (0.82)
  Pallas kernels: 163 us -> 141 us
  local copies, waits for them, and re-layouts: 11.8 us -> 0 us
    pallas_call x1 -> x2, Pallas kernels: 163 us -> 141 us  [the longest x1 139 us: local(): pl.pallas_call(kernel, out_shape=(pltpu.VMEM((TOK, KW), BF16), pltpu.VMEM...]
    unnamed x15 -> x0, local copies, waits for them, and re-layouts: 11 us -> none
where the time goes in v2:
time: 144 us; the launch traced here: 142 us
  Pallas kernels  141 us (98%)
    pallas_call x1, Pallas kernels, local(): pl.pallas_call(kernel, out_shape=(pltpu.VMEM((TOK, KW), BF16), pltpu.VMEM...  139 us

profile of v2, /device:TPU:1, one launch (start us, length us, event | category | flops | bytes accessed | tf_op | source)
XLA Modules:
  0.0 142.0 jit_solution(399922669513736355)
XLA Ops:
  0.6 139.3 %shard_map.118 = (bf16[256,512]{1,0:T(8,128)(2,1)S(1)}, bf16[2048,512]{1,0:T(8,128)(2,1)S(1)}, f32[112,128]{1,0:T(8,128)S(1)}, f32[112,128]{1,0:T(8,128)S(1)}, b...) custom-call(bf16[256,8192]{1,0:T(8,128)(2,1)} %act.1, bf16[2048,512]{1,0:T(8,128)(2,1)} %bitcast.5, ...), custom_call_target="tpu_custom_call" | custom-call | tf_op jit(solution)/shard_map/pallas_call | solution.py:336
  139.9 2.1 %shard_map.119 = (bf16[256,512]{1,0:T(8,128)(2,1)}, bf16[2048,512]{1,0:T(8,128)(2,1)}, f32[112,128]{1,0:T(8,128)}, f32[112,128]{1,0:T(8,128)}, bf16[4,4,4,112,12...) custom-call(bf16[256,512]{1,0:T(8,128)(2,1)S(1)} %get-tuple-element.18.key_v, ...), custom_call_target="tpu_custom_call" | custom-call | tf_op jit(solution)/shard_map/pallas_call | solution.py:384

commit v3 on v2

--- a/solution.py
+++ b/solution.py
@@ -11,12 +11,13 @@
 TOK, DEPTH, KW = 256, 2048, 512
 CODE_ROWS, OWN = 7168, 112
 QUARTER = CODE_ROWS // 4
-UNIT, WINDOW = 16, 2
+UNIT, EARLY, LATE, LAST, NARROW = 16, 4, 4, 3, 8
 NU = TOK // UNIT
-CHUNKS = ((0, 64), (64, 64), (128, 64), (192, 32), (224, 32))
+CHUNKS = ((0, 64), (64, 64), (128, 64), (192, 48), (240, 16))
 NQ = len(CHUNKS)
-ORDER = [*range(0, 4), "c", *range(4, NU)]
-PUMPS = (1, 0, 1, 2, 1, 1, 1, 1, 3, 0)
+HALVES = [(u, k) for u in range(NU) for k in range(2)]
+ORDER = HALVES[:8] + ["c"] + HALVES[8:]
+PUMPS = (2, 0, 2, 2, 2, 2, 1, 4, 4, 3, 3, 3)
 
 
 def kernel(
@@ -26,7 +27,7 @@
     p_loc, p_sib, p_rem, p_ex, ret_s, ret_r, grad_f,
     prod, recv_x, s_y, recv_y, s_z, recv_z,
     sem_in, sem_xs, sem_xr, sem_sib_s, sem_sib_r, sem_ex_s, sem_ex_r, sem_ret_s, sem_ret_r,
-    sem_rs_s, sem_rs_r, sem_ag_s, sem_ag_r,
+    sem_rs_s, sem_rs_r, sem_ag_s, sem_ag_r, token,
 ):
     r = lax.axis_index("replica")
     f = lax.axis_index("fsdp")
@@ -60,39 +61,47 @@
     in_master = local_copy(master, master_v, sem_in.at[5])
     in_momentum = local_copy(momentum, momentum_v, sem_in.at[6])
 
-    peers = [sib] + far + px + py + pz
+    rivals = [pz[1], (pz[1][0], far_same[1])]
+    peers = [sib] + far + px + py + pz + [rivals[1]]
     barrier = pltpu.get_barrier_semaphore()
     for peer in peers:
         pl.semaphore_signal(barrier, inc=1, device_id=peer, device_id_type=MESH)
     pl.semaphore_wait(barrier, len(peers))
 
-    far_x, far_c, issued = {}, [], []
-
-    def send_far(u):
-        if u == "c":
+    far_c, issued, sent = [], [], []
+
+    def send_far(item):
+        if item == "c":
             copy = remote(cot, c_rem.at[pl.ds(c * TOK, TOK)], sem_sib_s.at[2], sem_sib_r.at[2], far_same)
             far_c.append(copy)
-            return [copy]
+            return copy
+        u, k = item
         start, rows = next(chunk for chunk in CHUNKS if chunk[0] <= u * UNIT < sum(chunk))
-        copies = []
-        for k in range(2):
-            copies.append(remote(
-                act.at[pl.ds(u * UNIT, UNIT), columns((1 - zh) * 2 + k)],
-                x_rem.at[pl.ds(start + u * UNIT + c * rows, UNIT)],
-                sem_xs.at[2 * u + k], sem_xr.at[2 * u + c], far[k],
-            ))
-        return copies
-
-    def pump(steps):
-        for _ in range(steps):
-            if len(issued) == len(ORDER):
-                return
-            if len(issued) >= WINDOW:
-                for copy in issued[len(issued) - WINDOW]:
-                    copy.wait_send()
+        return remote(
+            act.at[pl.ds(u * UNIT, UNIT), columns((1 - zh) * 2 + k)],
+            x_rem.at[pl.ds(start + u * UNIT + c * rows, UNIT)],
+            sem_xs.at[2 * u + k], sem_xr.at[2 * u + c], far[k],
+        )
+
+    def step_done():
+        issued[len(sent)].wait_send()
+        sent.append(len(sent))
+        if len(sent) > len(ORDER) - LAST:
+            return
+        for i, peer in enumerate(rivals):
+            pl.semaphore_signal(token.at[i], inc=1, device_id=peer, device_id_type=MESH)
+        for i in range(2):
+            pl.semaphore_wait(token.at[i], 1)
+
+    def pump(steps, window=LATE):
+        for _ in range(min(steps, len(ORDER) - len(issued))):
+            if len(issued) >= len(ORDER) - NARROW:
+                window = LAST
+            while len(sent) + window <= len(issued):
+                step_done()
             issued.append(send_far(ORDER[len(issued)]))
 
-    pump(WINDOW)
+    pump(EARLY, EARLY)
     sib_x = remote(act.at[:, columns(zh * 2 + (1 - c))], x_loc.at[pl.ds(TOK, TOK)], sem_sib_s.at[0], sem_sib_r.at[0], sib)
     sib_c = remote(cot, c_loc.at[pl.ds(TOK, TOK)], sem_sib_s.at[1], sem_sib_r.at[1], sib)
 
@@ -115,9 +124,9 @@
         if k:
             rs_x.append(remote(prod.at[k], recv_x.at[k - 1], sem_rs_s.at[k - 1], sem_rs_r.at[k - 1], px[k - 1]))
         if k in (2, 3):
-            pump(PUMPS[0])
-
-    pump(PUMPS[1])
+            pump(PUMPS[0], EARLY)
+
+    pump(PUMPS[1], EARLY)
     in_x.wait()
     in_w.wait()
     in_c.wait()
@@ -132,7 +141,7 @@
     lax.fori_loop(0, 2 * TOK // 128, keys_local, 0)
     sib_p = remote(p_loc.at[pl.ds(TOK, TOK)], p_sib, sem_sib_s.at[3], sem_sib_r.at[3], sib)
 
-    pump(PUMPS[2])
+    pump(PUMPS[2], EARLY)
 
     def transposed_dot(lhs, rhs):
         return lax.dot_general(lhs, rhs, (((0,), (0,)), ((), ())), preferred_element_type=F32)
@@ -144,85 +153,7 @@
 
     lax.fori_loop(0, DEPTH // 256, grad_local, 0)
 
-    pump(PUMPS[3])
-    for copy in rs_x:
-        copy.wait()
-
-    def sum_x(b, carry):
-        at = pl.ds(pl.multiple_of(b * OWN, 16), OWN)
-        total = prod[0, at, :].astype(F32)
-        for k in range(3):
-            total += recv_x[k, at, :].astype(F32)
-        s_y[b // 4, b % 4] = total.astype(BF16)
-        return carry
-
-    lax.fori_loop(0, 16, sum_x, 0)
-    rs_y = [
-        remote(s_y.at[:, (y + k) % 4], recv_y.at[k - 1], sem_rs_s.at[2 + k], sem_rs_r.at[2 + k], py[k - 1])
-        for k in range(1, 4)
-    ]
-    pump(PUMPS[4])
-    for copy in rs_y:
-        copy.wait()
-
-    def sum_y(b, carry):
-        total = s_y[b, y].astype(F32)
-        for k in range(3):
-            total += recv_y[k, b].astype(F32)
-        s_z[b] = total.astype(BF16)
-        return carry
-
-    lax.fori_loop(0, 4, sum_y, 0)
-    rs_z = [
-        remote(s_z.at[(zl + k) % 4], recv_z.at[k - 1], sem_rs_s.at[5 + k], sem_rs_r.at[5 + k], pz[k - 1])
-        for k in range(1, 4)
-    ]
-    pump(PUMPS[5])
-    in_master.wait()
-    in_momentum.wait()
-    for copy in rs_z:
-        copy.wait()
-
-    total = s_z[zl].astype(F32)
-    for k in range(3):
-        total += recv_z[k].astype(F32)
-    outer = total / 64
-    new_momentum = 0.9 * momentum_v[...] + outer
-    new_master = master_v[...] - 0.7 * (outer + 0.9 * new_momentum)
-    nmom_v[...] = new_momentum
-    nm_v[...] = new_master
-    largest = jnp.max(jnp.abs(new_master), axis=1, keepdims=True)
-    scale = (largest + 1e-06).astype(BF16).astype(F32)
-    gath[x, zl, y, 0:OWN, :] = (new_master / scale).astype(BF16)
-    corner = lax.broadcasted_iota(jnp.int32, (OWN, 128), 0) == lax.broadcasted_iota(jnp.int32, (OWN, 128), 1)
-    row = jnp.sum(jnp.where(corner, jnp.broadcast_to(scale, (OWN, 128)), 0.0), axis=0, keepdims=True)
-    gath[x, zl, y, OWN:128, :] = jnp.broadcast_to(row, (128 - OWN, 128)).astype(BF16)
-
-    ag_z = [
-        remote(gath.at[x, zl, y], gath.at[x, zl, y], sem_ag_s.at[k - 1], sem_ag_r.at[k - 1], pz[k - 1])
-        for k in range(1, 4)
-    ]
-    pump(PUMPS[6])
-    for copy in ag_z:
-        copy.wait()
-    ag_y = [
-        remote(gath.at[x, :, y], gath.at[x, :, y], sem_ag_s.at[2 + k], sem_ag_r.at[2 + k], py[k - 1])
-        for k in range(1, 4)
-    ]
-    pump(PUMPS[7])
-    for copy in ag_y:
-        copy.wait()
-    ag_x = [
-        remote(gath.at[x], gath.at[x], sem_ag_s.at[5 + k], sem_ag_r.at[5 + k], px[k - 1])
-        for k in range(1, 4)
-    ]
-
-    pump(PUMPS[8])
-    far_c[0].wait_recv()
-    share_c = remote(
-        c_rem.at[pl.ds(c * TOK, TOK)], c_rem.at[pl.ds(c * TOK, TOK)], sem_sib_s.at[4], sem_sib_r.at[4], sib
-    )
-
+    pump(PUMPS[3], EARLY)
     def pack_scales():
         lane = lax.broadcasted_iota(jnp.int32, (1, 128), 1)
         for part in range(4):
@@ -242,7 +173,7 @@
     def keys_far(q):
         start, rows = CHUNKS[q]
         for u in range(start // UNIT, (start + rows) // UNIT):
-            while u not in [item for item in ORDER[:len(issued)]]:
+            while (u, 1) not in ORDER[: len(issued)]:
                 pump(1)
             for k in range(2):
                 part = x_rem.at[pl.ds(start + u * UNIT + k * rows, UNIT)]
@@ -277,31 +208,108 @@
 
         lax.fori_loop(0, DEPTH // 256, tile, 0)
 
-    exchange = keys_far(0)
+    for copy in rs_x:
+        copy.wait()
+
+    def sum_x(b, carry):
+        at = pl.ds(pl.multiple_of(b * OWN, 16), OWN)
+        total = prod[0, at, :].astype(F32)
+        for k in range(3):
+            total += recv_x[k, at, :].astype(F32)
+        s_y[b // 4, b % 4] = total.astype(BF16)
+        return carry
+
+    lax.fori_loop(0, 16, sum_x, 0)
+    rs_y = [
+        remote(s_y.at[:, (y + k) % 4], recv_y.at[k - 1], sem_rs_s.at[2 + k], sem_rs_r.at[2 + k], py[k - 1])
+        for k in range(1, 4)
+    ]
+    pump(PUMPS[4], EARLY)
+    for copy in rs_y:
+        copy.wait()
+
+    def sum_y(b, carry):
+        total = s_y[b, y].astype(F32)
+        for k in range(3):
+            total += recv_y[k, b].astype(F32)
+        s_z[b] = total.astype(BF16)
+        return carry
+
+    lax.fori_loop(0, 4, sum_y, 0)
+    rs_z = [
+        remote(s_z.at[(zl + k) % 4], recv_z.at[k - 1], sem_rs_s.at[5 + k], sem_rs_r.at[5 + k], pz[k - 1])
+        for k in range(1, 4)
+    ]
+    pump(PUMPS[5], EARLY)
+    in_master.wait()
+    in_momentum.wait()
+    for copy in rs_z:
+        copy.wait()
+
+    total = s_z[zl].astype(F32)
+    for k in range(3):
+        total += recv_z[k].astype(F32)
+    outer = total / 64
+    new_momentum = 0.9 * momentum_v[...] + outer
+    new_master = master_v[...] - 0.7 * (outer + 0.9 * new_momentum)
+    nmom_v[...] = new_momentum
+    nm_v[...] = new_master
+    largest = jnp.max(jnp.abs(new_master), axis=1, keepdims=True)
+    scale = (largest + 1e-06).astype(BF16).astype(F32)
+    gath[x, zl, y, 0:OWN, :] = (new_master / scale).astype(BF16)
+    corner = lax.broadcasted_iota(jnp.int32, (OWN, 128), 0) == lax.broadcasted_iota(jnp.int32, (OWN, 128), 1)
+    row = jnp.sum(jnp.where(corner, jnp.broadcast_to(scale, (OWN, 128)), 0.0), axis=0, keepdims=True)
+    gath[x, zl, y, OWN:128, :] = jnp.broadcast_to(row, (128 - OWN, 128)).astype(BF16)
+
+    ag_z = [
+        remote(gath.at[x, zl, y], gath.at[x, zl, y], sem_ag_s.at[k - 1], sem_ag_r.at[k - 1], pz[k - 1])
+        for k in range(1, 4)
+    ]
+    pump(PUMPS[6], EARLY)
+    returned = [keys_back(0, keys_far(0))]
+    for copy in ag_z:
+        copy.wait()
+    ag_y = [
+        remote(gath.at[x, :, y], gath.at[x, :, y], sem_ag_s.at[2 + k], sem_ag_r.at[2 + k], py[k - 1])
+        for k in range(1, 4)
+    ]
+    pump(PUMPS[7])
+    for copy in ag_y:
+        copy.wait()
+    ag_x = []
+
+    def gather_x(k):
+        ag_x.append(remote(gath.at[x], gath.at[x], sem_ag_s.at[5 + k], sem_ag_r.at[5 + k], px[k - 1]))
+
+    gather_x(2)
+    pump(PUMPS[8])
+    returned.append(keys_back(1, keys_far(1)))
+    gather_x(1)
+    far_c[0].wait_recv()
+    share_c = remote(
+        c_rem.at[pl.ds(c * TOK, TOK)], c_rem.at[pl.ds(c * TOK, TOK)], sem_sib_s.at[4], sem_sib_r.at[4], sib
+    )
+    pump(PUMPS[9])
     share_c.wait()
     for q, (start, rows) in enumerate(CHUNKS):
         for k in range(2):
             c_mix[pl.ds(2 * start + k * rows, rows), :] = c_rem[pl.ds(k * TOK + start, rows), :]
-    returned = []
-    pump(PUMPS[9])
-    for q in range(NQ):
-        if q == NQ - 2:
-            for copy in ag_x:
-                copy.wait()
-            pack_scales()
-        if q:
-            exchange = keys_far(q)
-        if q < NQ - 1:
-            grad_far(q)
-            pump(1)
-            returned.append(keys_back(q, exchange))
-            pump(1)
-    returned.append(keys_back(NQ - 1, exchange))
-    grad_far(NQ - 1)
-    for copies in issued[-WINDOW:]:
-        for copy in copies:
-            copy.wait_send()
+    grad_far(0)
+    pump(PUMPS[10])
+    gather_x(3)
+    grad_far(1)
+    pump(PUMPS[11])
+    returned.append(keys_back(2, keys_far(2)))
+    grad_far(2)
+    for q in range(3, NQ):
+        returned.append(keys_back(q, keys_far(q)))
+        grad_far(q)
+    while len(sent) < len(issued):
+        step_done()
     sib_p.wait()
+    for copy in ag_x:
+        copy.wait()
+    pack_scales()
 
     for q, (start, rows) in enumerate(CHUNKS):
         returned[q].wait()
@@ -376,6 +384,7 @@
             dma((NQ,)), dma((NQ,)),
             dma((9,)), dma((9,)),
             dma((9,)), dma((9,)),
+            pltpu.SemaphoreType.REGULAR((2,)),
         ],
         compiler_params=pltpu.CompilerParams(
             collective_id=0, has_side_effects=True, vmem_limit_bytes=58 * 2**20

time: 144 us -> 140 us (0.972)
  the two profiles are of different devices: /device:TPU:1 before, /device:TPU:42 now
where the time goes in v3:
time: 140 us
  Pallas kernels  140 us (100%)
    pallas_call x1, Pallas kernels, local(): pl.pallas_call(kernel, out_shape=(pltpu.VMEM((TOK, KW), BF16), pltpu.VMEM...  137 us

profile of v3, /device:TPU:42, one launch (start us, length us, event | category | flops | bytes accessed | tf_op | source)
XLA Modules:
  0.0 140.2 jit_solution(14349480187877628587)
XLA Ops:
  0.6 137.4 %shard_map.118 = (bf16[256,512]{1,0:T(8,128)(2,1)S(1)}, bf16[2048,512]{1,0:T(8,128)(2,1)S(1)}, f32[112,128]{1,0:T(8,128)S(1)}, f32[112,128]{1,0:T(8,128)S(1)}, b...) custom-call(bf16[256,8192]{1,0:T(8,128)(2,1)} %act.1, bf16[2048,512]{1,0:T(8,128)(2,1)} %bitcast.5, ...), custom_call_target="tpu_custom_call" | custom-call | tf_op jit(solution)/shard_map/pallas_call | solution.py:344
  138.1 2.1 %shard_map.119 = (bf16[256,512]{1,0:T(8,128)(2,1)}, bf16[2048,512]{1,0:T(8,128)(2,1)}, f32[112,128]{1,0:T(8,128)}, f32[112,128]{1,0:T(8,128)}, bf16[4,4,4,112,12...) custom-call(bf16[256,512]{1,0:T(8,128)(2,1)S(1)} %get-tuple-element.18.key_v, ...), custom_call_target="tpu_custom_call" | custom-call | tf_op jit(solution)/shard_map/pallas_call | solution.py:393

commit v4 on v3

--- a/solution.py
+++ b/solution.py
@@ -193,14 +193,13 @@
         ret_s[at, :] = (mine + p_ex[at, :]).astype(BF16)
         return remote(ret_s.at[at], ret_r.at[at], sem_ret_s.at[q], sem_ret_r.at[q], far_same)
 
-    def grad_far(q):
-        start, rows = CHUNKS[q]
-        both = pl.ds(2 * start, 2 * rows)
+    def grad_far(start, stop):
+        both = pl.ds(start, stop - start)
 
         def tile(b, carry):
             at = pl.ds(pl.multiple_of(b * 256, 256), 256)
             total = grad_f[at, :] + transposed_dot(x_rem[both, at], c_mix[both, :])
-            if q < NQ - 1:
+            if stop < 2 * TOK:
                 grad_f[at, :] = total
             else:
                 grad_b[at, :] = total.astype(BF16)
@@ -294,16 +293,14 @@
     for q, (start, rows) in enumerate(CHUNKS):
         for k in range(2):
             c_mix[pl.ds(2 * start + k * rows, rows), :] = c_rem[pl.ds(k * TOK + start, rows), :]
-    grad_far(0)
+    grad_far(0, 128)
     pump(PUMPS[10])
     gather_x(3)
-    grad_far(1)
+    grad_far(128, 256)
     pump(PUMPS[11])
-    returned.append(keys_back(2, keys_far(2)))
-    grad_far(2)
-    for q in range(3, NQ):
+    for q in range(2, NQ):
         returned.append(keys_back(q, keys_far(q)))
-        grad_far(q)
+    grad_far(256, 512)
     while len(sent) < len(issued):
         step_done()
     sib_p.wait()

time: 140 us -> 140 us (level)
  no operation moved by 1% of the time
where the time goes in v4:
time: 140 us
  Pallas kernels  139 us (99%)
    pallas_call x1, Pallas kernels, local(): pl.pallas_call(kernel, out_shape=(pltpu.VMEM((TOK, KW), BF16), pltpu.VMEM...  137 us

profile of v4, /device:TPU:42, one launch (start us, length us, event | category | flops | bytes accessed | tf_op | source)
XLA Modules:
  0.0 140.0 jit_solution(10946641904476266282)
XLA Ops:
  0.6 137.3 %shard_map.118 = (bf16[256,512]{1,0:T(8,128)(2,1)S(1)}, bf16[2048,512]{1,0:T(8,128)(2,1)S(1)}, f32[112,128]{1,0:T(8,128)S(1)}, f32[112,128]{1,0:T(8,128)S(1)}, b...) custom-call(bf16[256,8192]{1,0:T(8,128)(2,1)} %act.1, bf16[2048,512]{1,0:T(8,128)(2,1)} %bitcast.5, ...), custom_call_target="tpu_custom_call" | custom-call | tf_op jit(solution)/shard_map/pallas_call | solution.py:341
  137.9 2.1 %shard_map.119 = (bf16[256,512]{1,0:T(8,128)(2,1)}, bf16[2048,512]{1,0:T(8,128)(2,1)}, f32[112,128]{1,0:T(8,128)}, f32[112,128]{1,0:T(8,128)}, bf16[4,4,4,112,12...) custom-call(bf16[256,512]{1,0:T(8,128)(2,1)S(1)} %get-tuple-element.18.key_v, ...), custom_call_target="tpu_custom_call" | custom-call | tf_op jit(solution)/shard_map/pallas_call | solution.py:390
